TPU v7x, 768 devices: a whole 4x8x12 slice. The times are simulated.
768 devices in a mesh: space: 24 (over z, x_lo), dp: 32 (over x_hi, y, core).
Axes of the slice: x: 4 (x_hi: 2, x_lo: 2; x = x_hi * 2 + x_lo), y: 8, z: 12, core: 2. Of those that a mesh axis runs over, the one named last changes fastest.
Arguments:
- windows_in: bfloat16 [32, 192, 64, 768], P('dp', 'space'), may hold values from -6 to 6
- cotangent: bfloat16 [32, 192, 64, 768], P('dp', 'space'), may hold values from -0.1796875 to 0.1796875
- wet_mask: int32 [32, 192, 64], P('dp', 'space'), may hold values from 0 to 1, as said below
- wet_count: int32 [32, 24], P('dp', 'space'), may hold values from 1 to 8, as said below
- qkv_weight: bfloat16 [768, 1152], replicated, may hold values from -0.21875 to 0.21875
- proj_weight: bfloat16 [768, 384], replicated, may hold values from -0.3125 to 0.3125
- score_bias: float32 [6, 64, 64], replicated, may hold values from -4 to 256
Outputs:
- windows_out: bfloat16 [32, 192, 64, 768], P('dp', 'space')
- input_grad: bfloat16 [32, 192, 64, 768], P('dp', 'space')
- proj_grad: float32 [294912], P(('space', 'dp'))
Inputs may be any that keep to these rules, and one draw needn't show every extreme that they name: `wet_mask`: 1 marks a wet cell; every window slot has one or more wet cells. The wet windows of a tile fill its first slots; the later slots are land. Tiles t and t + 12 of a sample are matched partners: wet_count[b, t] + wet_count[b, t + 12] = 9.
All inputs are finite; a program needn't handle non-finite values.
Results may differ from a plain program's by a relative error of at most 0.0078.
Values may be sent and summed in bfloat16 or wider, within the bound.
No kernel may reach another device: no remote copies, remote signals or barrier semaphores. Data moves between devices by JAX's collectives and lax.ppermute only.
A program may use at most 32 MiB of HBM per device.

v0:
```python
import jax
import jax.numpy as jnp
from jax import lax
from jax.sharding import PartitionSpec as P

BLK_WIN = 4


epsilon = 1e-05


def window_pass(tile_x, tile_g, wet_cells, live_rows, qkv_weight, proj_weight, score_bias):
    head_count = score_bias.shape[0]
    cell_count = score_bias.shape[1]
    hidden_width = proj_weight.shape[1]
    head_size = hidden_width // head_count
    scale_factor = head_size ** (-0.5)
    window_count = tile_x.shape[0]
    split_shape = (window_count, cell_count, head_count, head_size)
    joined_shape = (window_count, cell_count, hidden_width)
    x_float = tile_x.astype(jnp.float32)
    centred = x_float - jnp.mean(x_float, -1, keepdims=True)
    inverse = lax.rsqrt(jnp.mean(centred * centred, -1, keepdims=True) + epsilon)
    normed = centred * inverse
    normed_low = normed.astype(jnp.bfloat16)
    mixed = jnp.einsum("wnc,ce->wne", normed_low, qkv_weight, preferred_element_type=jnp.float32)
    query = (mixed[..., :hidden_width] * scale_factor).astype(jnp.bfloat16).reshape(split_shape)
    keys_low = mixed[..., hidden_width : 2 * hidden_width].astype(jnp.bfloat16).reshape(split_shape)
    values_low = mixed[..., 2 * hidden_width :].astype(jnp.bfloat16).reshape(split_shape)
    scores = (
        jnp.einsum("wqhd,wkhd->whqk", query, keys_low, preferred_element_type=jnp.float32)
        + score_bias[None]
    )
    open_keys = (wet_cells > 0)[:, None, None, :]
    scores = jnp.where(open_keys, scores, -jnp.inf)
    raised = jnp.exp(scores - jnp.max(scores, -1, keepdims=True))
    probs = raised / jnp.sum(raised, -1, keepdims=True)
    probs_low = probs.astype(jnp.bfloat16)
    attended = jnp.einsum(
        "whqk,wkhd->wqhd", probs_low, values_low, preferred_element_type=jnp.float32
    )
    attended = attended.reshape(joined_shape).astype(jnp.bfloat16)
    branch = jnp.einsum("wne,ce->wnc", attended, proj_weight, preferred_element_type=jnp.float32)
    mask_rows = live_rows[:, None, None]
    windows_out = ((x_float + branch) * mask_rows).astype(jnp.bfloat16)
    grad_live = jnp.where(mask_rows > 0, tile_g, jnp.zeros_like(tile_g))
    proj_grad = jnp.einsum("wnc,wne->ce", grad_live, attended, preferred_element_type=jnp.float32)
    attended_grad = jnp.einsum(
        "wnc,ce->wne", grad_live, proj_weight, preferred_element_type=jnp.float32
    )
    attended_grad = attended_grad.astype(jnp.bfloat16).reshape(split_shape)
    probs_grad = jnp.einsum(
        "wqhd,wkhd->whqk", attended_grad, values_low, preferred_element_type=jnp.float32
    )
    values_grad = jnp.einsum(
        "whqk,wqhd->wkhd", probs_low, attended_grad, preferred_element_type=jnp.float32
    )
    score_grad = probs * (probs_grad - jnp.sum(probs * probs_grad, -1, keepdims=True))
    score_grad = score_grad.astype(jnp.bfloat16)
    query_grad = (
        jnp.einsum("whqk,wkhd->wqhd", score_grad, keys_low, preferred_element_type=jnp.float32)
        * scale_factor
    )
    keys_grad = jnp.einsum("whqk,wqhd->wkhd", score_grad, query, preferred_element_type=jnp.float32)
    mixed_grad = jnp.concatenate(
        [
            query_grad.reshape(joined_shape),
            keys_grad.reshape(joined_shape),
            values_grad.reshape(joined_shape),
        ],
        -1,
    )
    mixed_grad = mixed_grad.astype(jnp.bfloat16)
    normed_grad = jnp.einsum(
        "wne,ce->wnc", mixed_grad, qkv_weight, preferred_element_type=jnp.float32
    )
    branch_grad = inverse * (
        normed_grad
        - jnp.mean(normed_grad, -1, keepdims=True)
        - normed * jnp.mean(normed_grad * normed, -1, keepdims=True)
    )
    input_grad = (grad_live.astype(jnp.float32) + branch_grad).astype(jnp.bfloat16)
    return (windows_out, input_grad, proj_grad)


def run_windows(buffer_x, buffer_g, buffer_wet, live_total, weights):
    qkv_weight, proj_weight, score_bias = weights
    block_total = (live_total + BLK_WIN - 1) // BLK_WIN

    def one_block(block_index, running):
        out_buffer, grad_buffer, proj_sum = running
        first_slot = block_index * BLK_WIN
        block_x = lax.dynamic_slice_in_dim(buffer_x, first_slot, BLK_WIN, 0)
        block_g = lax.dynamic_slice_in_dim(buffer_g, first_slot, BLK_WIN, 0)
        block_wet = lax.dynamic_slice_in_dim(buffer_wet, first_slot, BLK_WIN, 0)
        live_rows = (first_slot + jnp.arange(BLK_WIN, dtype=jnp.int32) < live_total).astype(
            jnp.float32
        )
        result, grads_in, proj_part = window_pass(
            block_x, block_g, block_wet, live_rows, qkv_weight, proj_weight, score_bias
        )
        out_buffer = lax.dynamic_update_slice_in_dim(out_buffer, result, first_slot, 0)
        grad_buffer = lax.dynamic_update_slice_in_dim(grad_buffer, grads_in, first_slot, 0)
        return (out_buffer, grad_buffer, proj_sum + proj_part)

    initial = (
        jnp.zeros_like(buffer_x),
        jnp.zeros_like(buffer_x),
        jnp.zeros(proj_weight.shape, jnp.float32),
    )
    return lax.fori_loop(0, block_total, one_block, initial)


def shards(windows_in, cotangent, wet_mask, wet_count, qkv_weight, proj_weight, score_bias):
    tile_x = windows_in[0]
    tile_g = cotangent[0]
    wet_cells = wet_mask[0]
    own_count = wet_count[0, 0]
    weights = (qkv_weight, proj_weight, score_bias)
    out_tile, grad_tile, proj_sum = run_windows(tile_x, tile_g, wet_cells, own_count, weights)
    flat_proj = proj_sum.reshape(-1)
    summed_proj = lax.psum_scatter(flat_proj, ("space", "dp"), scatter_dimension=0, tiled=True)
    return (out_tile[None], grad_tile[None], summed_proj)


def solution(mesh):
    in_specs = (
        P("dp", "space", None, None),
        P("dp", "space", None, None),
        P("dp", "space", None),
        P("dp", "space"),
        P(),
        P(),
        P(),
    )
    out_specs = (P("dp", "space", None, None), P("dp", "space", None, None), P(("space", "dp")))
    return jax.shard_map(shards, mesh=mesh, in_specs=in_specs, out_specs=out_specs, check_vma=False)
```

profile of v0, /device:TPU:1, one launch (start us, length us, event | category | flops | bytes accessed | tf_op | source)
XLA Modules:
  0.0 549.0 jit_solution(74958309226879546)
XLA Ops:
  7.2 0.0 all-reduce.3.cloned.1.call-start
  7.9 1.0 copy.63
  8.9 0.9 broadcast.80
  9.9 0.9 broadcast.80.clone
  10.8 1.1 broadcast_in_dim.36
  11.9 0.0 copy-done
  11.9 25.7 %while.14 = (s32[]{:T(128)}, bf16[8,64,768]{2,1,0:T(8,128)(2,1)}, bf16[8,64,768]{2,1,0:T(8,128)(2,1)}, f32[768,384]{1,0:T(8,128)}, s32[]{:T(128)}, /*index=5*/bf...) while((s32[]{:T(128)}, bf16[8,64,768]{2,1,0:T(8,128)(2,1)}, ...), condition=%wide.region_8.9_spmd, body=%wide.region_0.8_spmd.sunk | while | flops 1445759232 | bytes 52093660 | solution.py:111
  11.9 0.1 convert_reduce_fusion.2
  12.1 0.2 fusion.108
  12.3 0.0 copy-start.12
  12.3 2.2 fusion.109
  14.6 1.1 reshape.75
  15.8 0.2 copy.89
  16.0 0.2 copy.90
  16.3 0.7 dynamic-slice_compare_fusion.2
  17.0 0.3 fusion.112
  17.3 1.3 fusion.113
  18.5 1.4 convolution_convert_fusion.8
  20.0 0.0 copy-start.3
  20.0 0.0 copy-start.5
  20.0 0.8 broadcast_compare_fusion.2
  20.8 0.0 copy-start.14
  20.8 2.4 fusion.114
  23.2 1.1 convolution_convert_fusion.9
  24.3 1.9 copy.91
  26.1 2.1 convolution_convert_fusion.10
  28.2 1.2 copy.92
  29.4 1.4 multiply_reduce_fusion.2
  30.8 0.2 multiply_convert_fusion.2
  31.0 0.3 convolution_convert_fusion.11
  31.4 0.0 copy-start.9
  31.4 0.0 copy-start.13
  31.4 0.2 copy.93
  31.6 0.2 fusion.115
  31.8 0.2 copy.94
  32.0 0.0 copy-done.9
  32.0 0.0 copy-done.13
  32.1 2.4 fusion.116
  34.5 0.4 fusion.117
  34.9 0.0 copy-start.11
  34.9 0.8 copy-done.1
  35.8 0.8 fusion.118
  36.6 1.0 copy-done.2
  37.6 0.0 copy-done.7
  37.6 2.4 reshape.70
  40.0 0.0 all-reduce.3.cloned.1.call-update
  40.0 500.9 %all-reduce.3.cloned.1.call-done = f32[294912]{0:T(1024)} async-done(((f32[294912]{0:T(1024)}), f32[294912]{0:T(1024)}) %all-reduce.3.cloned.1.call-update) | async-done | bytes 1179664
  540.8 1.3 dynamic-slice
  (24 shorter events, 0.1 us)
Async XLA Ops:
  7.2 533.7 %all-reduce.3.cloned.1.call-start = ((), (), s32[]{:S(2)}) async-start(), calls=%async_computation | async-start | bytes 2359296
  9.9 2.0 copy-start
  11.9 5.1 copy-start.6
  12.0 2.5 copy-start.8
  12.3 2.3 copy-start.12
  20.0 3.2 copy-start.3
  20.0 3.2 copy-start.5
  20.8 2.4 copy-start.14
  31.4 0.7 copy-start.9
  31.4 0.7 copy-start.13
  32.1 2.4 copy-start.4
  32.1 2.5 copy-start.10
  32.1 2.5 copy-start.15
  34.5 1.3 copy-start.1
  34.9 1.7 copy-start.11
  35.7 1.8 copy-start.7
  36.6 1.0 copy-start.2
Sparse Core Ops, SparseCore 0:
  40.1 500.6 all-reduce.2
where the time goes:
time: 550 us; the launch traced here: 549 us
  waiting for transfers between devices  501 us (91%)
  matrix products  14.8 us (3%)
  between operations  14.7 us (3%)
  local copies, waits for them, and re-layouts  14.6 us (3%)
    unnamed x2, waiting for transfers between devices  501 us
  transfers between devices with their start and end apart: 1, of which 1 were waited for; matrix products, arithmetic and copies ran while one was open for 0% of the time, Pallas kernels for 0%

commit v1 on v0

v1 whole, which is shorter than its diff:
```python
import functools
import jax
import jax.numpy as jnp
from jax import lax
from jax.experimental import pallas as pl
from jax.experimental.pallas import tpu as pltpu
from jax.sharding import PartitionSpec as P

EPSILON = 1e-05
PAIR = 128
VMEM_BYTES = 58 * 1024 * 1024
BF16 = jnp.bfloat16
F32 = jnp.float32


def dot(lhs, rhs, lhs_axis, rhs_axis):
    return lax.dot_general(
        lhs, rhs, (((lhs_axis,), (rhs_axis,)), ((), ())), preferred_element_type=F32
    )


def make_spread(cells, size):
    same_head = (
        lax.broadcasted_iota(jnp.int32, (PAIR, PAIR), 0) // size
        == lax.broadcasted_iota(jnp.int32, (PAIR, PAIR), 1) // size
    )
    first_head = lax.broadcasted_iota(jnp.int32, (cells, PAIR), 1) < size

    def spread(low):
        return jnp.where(same_head, jnp.concatenate([low, low], 0), jnp.zeros((), BF16))

    def own(both):
        return jnp.where(first_head, both[:cells], both[cells:])

    return spread, own


def keep_live(ref, count_ref, cells):
    live = lax.broadcasted_iota(jnp.int32, (ref.shape[0], 1), 0) < count_ref[0, 0] * cells
    ref[...] = jnp.where(live, ref[...], jnp.zeros((), BF16))


class Fetch:
    def __init__(self, sems):
        self.sems = sems
        self.used = 0

    def __call__(self, source, target):
        copy = pltpu.make_async_copy(source, target, self.sems.at[self.used])
        self.used += 1
        copy.start()
        return copy


def attend(
    wet_ref, bias_ref, x_ref, qkv_ref, mixed_ref, attended_ref, probs_ref, probs_low_ref, scores_ref, bias_t_ref,
    normed_ref, inverse_ref, x_wait, small_waits, qkv_wait, sizes,
):
    windows, cells, heads = sizes
    hidden = attended_ref.shape[1]
    size = hidden // heads
    pairs = hidden // PAIR
    scale = size ** (-0.5)
    spread, own = make_spread(cells, size)

    x_wait()
    x_float = x_ref[...].astype(F32)
    centred = x_float - jnp.mean(x_float, -1, keepdims=True)
    inverse = lax.rsqrt(jnp.mean(centred * centred, -1, keepdims=True) + EPSILON)
    normed = centred * inverse
    if normed_ref is not None:
        normed_ref[...] = normed
        inverse_ref[...] = inverse
    normed_low = normed.astype(BF16)
    small_waits()
    bias_t_ref[...] = bias_ref[...].T
    closed = jnp.where(wet_ref[...] > 0, 0.0, -jnp.inf).astype(F32).T
    qkv_wait()
    for part in range(3):
        lanes = slice(part * hidden, (part + 1) * hidden)
        mixed = dot(normed_low, qkv_ref[:, lanes], 1, 0)
        if part == 0:
            mixed = mixed * scale
        mixed_ref[:, lanes] = mixed.astype(BF16)

    for window in range(windows):
        at = slice(window * cells, (window + 1) * cells)
        for pair in range(pairs):
            lanes = slice(pair * PAIR, (pair + 1) * PAIR)
            query = mixed_ref[at, lanes]
            keys = mixed_ref[at, hidden + pair * PAIR : hidden + (pair + 1) * PAIR]
            scores = dot(keys, spread(query), 1, 1) + bias_t_ref[:, lanes]
            scores_ref[at, lanes] = scores + closed[:, window : window + 1]
    for window in range(windows):
        at = slice(window * cells, (window + 1) * cells)
        scores = scores_ref[at, :]
        raised = jnp.exp(scores - jnp.max(scores, 0, keepdims=True))
        probs = raised * (1.0 / jnp.sum(raised, 0, keepdims=True))
        probs_low_ref[at, :] = probs.astype(BF16)
        if probs_ref is not None:
            probs_ref[at, :] = probs
    for window in range(windows):
        at = slice(window * cells, (window + 1) * cells)
        for pair in range(pairs):
            lanes = slice(pair * PAIR, (pair + 1) * PAIR)
            values = mixed_ref[at, 2 * hidden + pair * PAIR : 2 * hidden + (pair + 1) * PAIR]
            attended_ref[at, lanes] = own(dot(probs_low_ref[at, lanes], values, 0, 0)).astype(BF16)


def share_kernel(
    wet_hbm, bias_hbm, count_ref, x_hbm, g_hbm, qkv_hbm, share_ref,
    wet_ref, bias_ref, x_ref, g_ref, qkv_ref, mixed_ref, attended_ref, bias_t_ref, probs_low_ref, scores_ref,
    lines_ref, sems, *, sizes, outer, inner,
):
    rows, width = x_ref.shape
    cells = sizes[1]
    pairs = attended_ref.shape[1] // PAIR
    fetch = Fetch(sems)
    x_copy = fetch(x_hbm, x_ref)
    bias_copy = fetch(bias_hbm, bias_ref)
    wet_copy = fetch(wet_hbm, wet_ref)
    qkv_copy = fetch(qkv_hbm, qkv_ref)
    g_copy = fetch(g_hbm, g_ref)

    def small_waits():
        bias_copy.wait()
        wet_copy.wait()

    attend(
        wet_ref, bias_ref, x_ref, qkv_ref, mixed_ref, attended_ref, None, probs_low_ref, scores_ref, bias_t_ref,
        None, None, x_copy.wait, small_waits, qkv_copy.wait, sizes,
    )
    g_copy.wait()
    keep_live(g_ref, count_ref, cells)
    total = dot(g_ref[...], attended_ref[...], 0, 0)
    for k in range(pairs):
        part = total[:, k * PAIR : (k + 1) * PAIR].reshape(outer, inner, PAIR)
        part = jnp.transpose(part, (1, 0, 2)).reshape(inner // 2, 2, outer, PAIR)
        for core in range(2):
            lines = pl.ds(core * width * pairs // 2 + k, width // 2, stride=pairs)
            lines_ref[lines, :] = part[:, core].reshape(width // 2, PAIR)
    share_ref[...] = lines_ref[...].astype(BF16).reshape(share_ref.shape)


def grads_kernel(
    wet_hbm, bias_hbm, count_ref, x_hbm, g_hbm, qkv_hbm, proj_hbm, out_hbm, grad_hbm,
    wet_ref, bias_ref, x_ref, g_ref, qkv_ref, proj_ref, mixed_ref, attended_ref, bias_t_ref, probs_low_ref, scores_ref,
    probs_ref, normed_ref, inverse_ref, agrad_ref, mgrad_ref, out_ref, grad_ref,
    sems, *, sizes,
):
    windows, cells, heads = sizes
    rows, width = x_ref.shape
    hidden = proj_ref.shape[1]
    size = hidden // heads
    pairs = hidden // PAIR
    scale = size ** (-0.5)
    spread, own = make_spread(cells, size)
    fetch = Fetch(sems)
    x_copy = fetch(x_hbm, x_ref)
    bias_copy = fetch(bias_hbm, bias_ref)
    wet_copy = fetch(wet_hbm, wet_ref)
    qkv_copy = fetch(qkv_hbm, qkv_ref)
    g_copy = fetch(g_hbm, g_ref)
    proj_copy = fetch(proj_hbm, proj_ref)

    def small_waits():
        bias_copy.wait()
        wet_copy.wait()

    attend(
        wet_ref, bias_ref, x_ref, qkv_ref, mixed_ref, attended_ref, probs_ref, probs_low_ref, scores_ref, bias_t_ref,
        normed_ref, inverse_ref, x_copy.wait, small_waits, qkv_copy.wait, sizes,
    )
    g_copy.wait()
    keep_live(g_ref, count_ref, cells)
    proj_copy.wait()
    branch = dot(attended_ref[...], proj_ref[...], 1, 1)
    out_ref[...] = (x_ref[...].astype(F32) + branch).astype(BF16)
    keep_live(out_ref, count_ref, cells)
    out_copy = fetch(out_ref, out_hbm)
    agrad_ref[...] = dot(g_ref[...], proj_ref[...], 1, 0).astype(BF16)

    for window in range(windows):
        at = slice(window * cells, (window + 1) * cells)
        for pair in range(pairs):
            lanes = slice(pair * PAIR, (pair + 1) * PAIR)
            value_lanes = slice(2 * hidden + pair * PAIR, 2 * hidden + (pair + 1) * PAIR)
            agrad = spread(agrad_ref[at, lanes])
            scores_ref[at, lanes] = dot(mixed_ref[at, value_lanes], agrad, 1, 1)
            mgrad_ref[at, value_lanes] = dot(probs_low_ref[at, lanes], agrad, 1, 0).astype(BF16)
    for window in range(windows):
        at = slice(window * cells, (window + 1) * cells)
        probs = probs_ref[at, :]
        probs_grad = scores_ref[at, :]
        score_grad = probs * (probs_grad - jnp.sum(probs * probs_grad, 0, keepdims=True))
        probs_low_ref[at, :] = score_grad.astype(BF16)
    for window in range(windows):
        at = slice(window * cells, (window + 1) * cells)
        for pair in range(pairs):
            lanes = slice(pair * PAIR, (pair + 1) * PAIR)
            key_lanes = slice(hidden + pair * PAIR, hidden + (pair + 1) * PAIR)
            score_grad = probs_low_ref[at, lanes]
            query_grad = own(dot(score_grad, mixed_ref[at, key_lanes], 0, 0)) * scale
            mgrad_ref[at, lanes] = query_grad.astype(BF16)
            keys_grad = dot(score_grad, spread(mixed_ref[at, lanes]), 1, 0)
            mgrad_ref[at, key_lanes] = keys_grad.astype(BF16)

    normed_grad = dot(mgrad_ref[...], qkv_ref[...], 1, 1)
    normed = normed_ref[...]
    branch_grad = inverse_ref[...] * (
        normed_grad
        - jnp.mean(normed_grad, -1, keepdims=True)
        - normed * jnp.mean(normed_grad * normed, -1, keepdims=True)
    )
    grad_ref[...] = (g_ref[...].astype(F32) + branch_grad).astype(BF16)
    grad_copy = fetch(grad_ref, grad_hbm)
    out_copy.wait()
    grad_copy.wait()


def staging(x, g, wet, count, qkv_weight, score_bias):
    windows, cells, width = x.shape
    heads = score_bias.shape[0]
    hidden = qkv_weight.shape[1] // 3
    rows = windows * cells
    staged = [
        pltpu.VMEM((windows, cells), jnp.int32),
        pltpu.VMEM((heads * cells, cells), F32),
        pltpu.VMEM((rows, width), BF16),
        pltpu.VMEM((rows, width), BF16),
        pltpu.VMEM((width, 3 * hidden), BF16),
    ]
    worked = [
        pltpu.VMEM((rows, 3 * hidden), BF16),
        pltpu.VMEM((rows, hidden), BF16),
        pltpu.VMEM((cells, hidden), F32),
        pltpu.VMEM((rows, hidden), BF16),
        pltpu.VMEM((rows, hidden), F32),
    ]
    args = (
        wet,
        score_bias.reshape(heads * cells, cells),
        count,
        x.reshape(rows, width),
        g.reshape(rows, width),
        qkv_weight,
    )
    return args, staged, worked, (windows, cells, heads)


def placed(arrays):
    specs = [pl.BlockSpec(memory_space=pltpu.HBM)] * arrays
    return specs[:2] + [pl.BlockSpec(memory_space=pltpu.SMEM)] + specs[2:]


def share_call(x, g, wet, count, qkv_weight, score_bias, outer, inner):
    args, staged, worked, sizes = staging(x, g, wet, count, qkv_weight, score_bias)
    rows, width = args[3].shape
    hidden = qkv_weight.shape[1] // 3
    pairs = hidden // PAIR
    return pl.pallas_call(
        functools.partial(share_kernel, sizes=sizes, outer=outer, inner=inner),
        out_shape=jax.ShapeDtypeStruct((2, inner // 2, outer * pairs, PAIR), BF16),
        in_specs=placed(5),
        out_specs=pl.BlockSpec(memory_space=pltpu.VMEM),
        scratch_shapes=staged
        + worked
        + [
            pltpu.VMEM((width * pairs, PAIR), F32),
            pltpu.SemaphoreType.DMA((5,)),
        ],
        compiler_params=pltpu.CompilerParams(vmem_limit_bytes=VMEM_BYTES),
        cost_estimate=pl.CostEstimate(
            flops=2 * rows * width * 4 * hidden, bytes_accessed=4_000_000, transcendentals=200_000
        ),
    )(*args)


def grads_call(x, g, wet, count, qkv_weight, proj_weight, score_bias):
    args, staged, worked, sizes = staging(x, g, wet, count, qkv_weight, score_bias)
    rows, width = args[3].shape
    hidden = proj_weight.shape[1]
    hbm = pl.BlockSpec(memory_space=pltpu.HBM)
    flat = jax.ShapeDtypeStruct((rows, width), BF16)
    return pl.pallas_call(
        functools.partial(grads_kernel, sizes=sizes),
        out_shape=(flat, flat),
        in_specs=placed(6),
        out_specs=(hbm, hbm),
        scratch_shapes=staged
        + [pltpu.VMEM((width, hidden), BF16)]
        + worked
        + [
            pltpu.VMEM((rows, hidden), F32),
            pltpu.VMEM((rows, width), F32),
            pltpu.VMEM((rows, 1), F32),
            pltpu.VMEM((rows, hidden), BF16),
            pltpu.VMEM((rows, 3 * hidden), BF16),
            pltpu.VMEM((rows, width), BF16),
            pltpu.VMEM((rows, width), BF16),
            pltpu.SemaphoreType.DMA((8,)),
        ],
        compiler_params=pltpu.CompilerParams(vmem_limit_bytes=VMEM_BYTES),
        cost_estimate=pl.CostEstimate(
            flops=2 * rows * width * 16 * hidden, bytes_accessed=30_000_000, transcendentals=200_000
        ),
    )(*args, proj_weight)


def block_call(x, g, wet, count, qkv_weight, proj_weight, score_bias, outer, inner):
    share = share_call(x, g, wet, count, qkv_weight, score_bias, outer, inner)
    out, grad = grads_call(x, g, wet, count, qkv_weight, proj_weight, score_bias)
    return out, grad, share


def shards(windows_in, cotangent, wet_mask, wet_count, qkv_weight, proj_weight, score_bias):
    outer, inner = lax.axis_size("space"), lax.axis_size("dp")
    pairs = proj_weight.shape[1] // PAIR
    x, g = windows_in[0], cotangent[0]
    wet, count = wet_mask[0], wet_count
    share = share_call(x, g, wet, count, qkv_weight, score_bias, outer, inner)
    pairs_of_cores = [(i, i ^ 1) for i in range(inner)]
    core = lax.rem(lax.axis_index("dp"), 2)
    sent = lax.dynamic_index_in_dim(share, 1 - core, 0, keepdims=False)
    held = lax.dynamic_index_in_dim(share, core, 0, keepdims=False)
    got = lax.ppermute(sent, "dp", pairs_of_cores)
    share = (held.astype(F32) + got.astype(F32)).astype(BF16)
    wet, share = lax.optimization_barrier((wet, share))
    groups = [list(range(core, inner, 2)) for core in range(2)]
    got = lax.all_to_all(share, "dp", 0, 0, tiled=True, axis_index_groups=groups)
    out, grad = grads_call(x, g, wet, count, qkv_weight, proj_weight, score_bias)
    got, out, grad = lax.optimization_barrier((got, out, grad))
    part = jnp.sum(got.astype(F32), 0).astype(BF16).reshape(outer, pairs, PAIR)
    got = lax.all_to_all(part, "space", 0, 0, tiled=True)
    total = jnp.sum(got.astype(F32), 0).reshape(-1)
    return (out.reshape(windows_in.shape), grad.reshape(windows_in.shape), total)


def solution(mesh):
    in_specs = (
        P("dp", "space", None, None),
        P("dp", "space", None, None),
        P("dp", "space", None),
        P("dp", "space"),
        P(),
        P(),
        P(),
    )
    out_specs = (P("dp", "space", None, None), P("dp", "space", None, None), P(("space", "dp")))
    return jax.shard_map(shards, mesh=mesh, in_specs=in_specs, out_specs=out_specs, check_vma=False)
```

time: 550 us -> 62.7 us (0.11)
  the two profiles are of different devices: /device:TPU:1 before, /device:TPU:8 now
where the time goes in v1:
time: 62.7 us; the launch traced here: 62.3 us
  blocking collectives  23.2 us (37%)
  Pallas kernels  14.7 us (23%)
  starting transfers between devices  14.7 us (23%)
  waiting for transfers between devices  5 us (8%)
  other arithmetic  2.41 us (4%)
  between operations  1.32 us (2%)
  local copies, waits for them, and re-layouts  1.01 us (2%)
    all_to_all x1, blocking collectives, shards(): got = lax.all_to_all(part, 'space', 0, 0, tiled=True)  23.2 us
    all_to_all x1, starting transfers between devices, shards(): lax.all_to_all(share, 'dp', 0, 0, tiled=True, axis_index_groups=groups)  12.8 us
    pallas_call x1, Pallas kernels, grads_call(): pl.pallas_call(functools.partial(grads_kernel, sizes=sizes), out_shape=(f...  9.12 us
    pallas_call x1, Pallas kernels, share_call(): pl.pallas_call(functools.partial(share_kernel, sizes=sizes, outer=outer,...  5.58 us
    all_to_all x1, waiting for transfers between devices, shards(): lax.all_to_all(share, 'dp', 0, 0, tiled=True, axis_index_groups=groups)  3.46 us
    ppermute x1, starting transfers between devices, shards(): got = lax.ppermute(sent, 'dp', pairs_of_cores)  1.92 us
    convert_element_type x1, other arithmetic, shards(): share = (held.astype(F32) + got.astype(F32)).astype(BF16)  1.75 us
    ppermute x1, waiting for transfers between devices, shards(): got = lax.ppermute(sent, 'dp', pairs_of_cores)  1.54 us
  transfers between devices with their start and end apart: 2, of which 2 were waited for; matrix products, arithmetic and copies ran while one was open for 0% of the time, Pallas kernels for 15%

profile of v1, /device:TPU:8, one launch (start us, length us, event | category | flops | bytes accessed | tf_op | source)
XLA Modules:
  0.0 62.3 jit_solution(15237234861320728600)
XLA Ops:
  1.3 5.6 %shard_map.94 = bf16[2,16,72,128]{3,2,1,0:T(8,128)(2,1)} custom-call(s32[8,64]{1,0:T(8,128)} %bitcast.19, f32[384,64]{1,0:T(8,128)} %bitcast.17, s32[1,1]{1,0:T(1,128)S(6)} %copy.10.count_ref, bf16[512,768]{1,0:T(8,128)(2,1)} %bitcast.13, bf16[512,768]{1,0:T(8,128)(2,1)} %bitcast.15, bf16[768,1152]{1,0:T(8,128)(2,1)} %qkv_hbm.3), custom_call_target="tpu_custom_call" | custom-call | flops 1207959552 | bytes 4000000 | tf_op jit(solution)/shard_map/pallas_call | solution.py:261
  6.9 1.0 %dynamic-slice_bitcast_fusion = bf16[16,72,128]{2,1,0:T(8,128)(2,1)S(1)} fusion(bf16[2,16,72,128]{3,2,1,0:T(8,128)(2,1)} %shard_map.94, s32[]{:T(128)S(6)} %select_n.8), kind=kLoop, calls=%fused_computation.2 | loop fusion | bytes 589828 | tf_op jit(solution)/shard_map/jit(dynamic_index_in_dim)/squeeze | solution.py:324
  7.9 1.9 %collective-permute-start = (bf16[16,72,128]{2,1,0:T(8,128)(2,1)S(1)}, bf16[16,72,128]{2,1,0:T(8,128)(2,1)S(1)}, u32[]{:S(2)}, u32[]{:S(2)}) collective-permute-start(bf16[16,72,128]{2,1,0:T(8,128)(2,1)S(1)} %dynamic-slice_bitcast_fusion), channel_id=1, source_target_pairs={{0,1},{1,0},{2,3},{3,2},{4,5},{5,4},{6,7},{7,6},{8,9},{9,8},{10,11... | collective-permute-start | bytes 884744 | tf_op jit(solution)/shard_map/ppermute | solution.py:326
  9.8 1.5 %collective-permute-done = bf16[16,72,128]{2,1,0:T(8,128)(2,1)S(1)} collective-permute-done((bf16[16,72,128]{2,1,0:T(8,128)(2,1)S(1)}, bf16[16,72,128]{2,1,0:T(8,128)(2,1)S(1)}, u32[]{:S(2)}, u32[]{:S(2)}) %collective-permute-start) | collective-permute-done | bytes 294944 | tf_op jit(solution)/shard_map/ppermute | solution.py:326
  11.3 1.7 %fusion = bf16[16,72,128]{2,1,0:T(8,128)(2,1)} fusion(bf16[16,72,128]{2,1,0:T(8,128)(2,1)S(1)} %collective-permute-done, bf16[2,16,72,128]{3,2,1,0:T(8,128)(2,1)} %shard_map.94, s32[]{:T(128)S(6)} %select_n.7), kind=kLoop, calls=%fused_computation.1 | loop fusion | flops 589824 | bytes 884740 | tf_op jit(solution)/shard_map/convert_element_type | solution.py:327
  13.1 12.8 %all-to-all-start = ((bf16[16,72,128]{2,1,0:T(8,128)(2,1)}), bf16[16,72,128]{2,1,0:T(8,128)(2,1)S(1)}, u32[]{:S(2)}, u32[]{:S(2)}) async-start(bf16[16,72,128]{2,1,0:T(8,128)(2,1)} %fusion), calls=%async_computation | async-start | bytes 589824 | tf_op jit(solution)/shard_map/all_to_all | solution.py:330
  25.9 9.1 %shard_map.95 = (bf16[512,768]{1,0:T(8,128)(2,1)}, bf16[512,768]{1,0:T(8,128)(2,1)}) custom-call(s32[8,64]{1,0:T(8,128)} %bitcast.20, f32[384,64]{1,0:T(8,128)} %bitcast.18, s32[1,1]{1,0:T(1,128)S(6)} %copy.10.count_ref, bf16[512,768]{1,0:T(8,128)(2,1)} %bitcast.14, bf16[512,768]{1,0:T(8,128)(2,1)} %bitcast.16, bf16[768,1152]{1,0:T(8,128)(2,1)} %qkv_hbm.3, ...), custom_call_target="tpu_custom_call" | custom-call | flops 4831838208 | bytes 30000000 | tf_op jit(solution)/shard_map/pallas_call | solution.py:285
  35.0 3.5 %all-to-all-done = bf16[16,72,128]{2,1,0:T(8,128)(2,1)S(1)} async-done(((bf16[16,72,128]{2,1,0:T(8,128)(2,1)}), bf16[16,72,128]{2,1,0:T(8,128)(2,1)S(1)}, u32[]{:S(2)}, u32[]{:S(2)}) %all-to-all-start) | async-done | bytes 294944 | tf_op jit(solution)/shard_map/all_to_all | solution.py:330
  38.5 23.2 %all_to_all.10 = bf16[24,3,128]{2,1,0:T(4,128)(2,1)S(1)} all-to-all(bf16[24,3,128]{2,1,0:T(4,128)(2,1)S(1)} %reshape.27), channel_id=1, replica_groups=mesh['space'=24,'dp'=32] {'space'}, dimensions={0} | all-to-all | bytes 36864 | tf_op jit(solution)/shard_map/all_to_all | solution.py:334
  61.7 0.6 convert_reduce_fusion
  (2 shorter events, 0.1 us)
Async XLA Ops:
  7.9 3.5 %collective-permute-start = (bf16[16,72,128]{2,1,0:T(8,128)(2,1)S(1)}, bf16[16,72,128]{2,1,0:T(8,128)(2,1)S(1)}, u32[]{:S(2)}, u32[]{:S(2)}) collective-permute-start(bf16[16,72,128]{2,1,0:T(8,128)(2,1)S(1)} %dynamic-slice_bitcast_fusion), channel_id=1, source_target_pairs={{0,1},{1,0},{2,3},{3,2},{4,5},{5,4},{6,7},{7,6},{8,9},{9,8},{10,11... | collective-permute-start | bytes 884744 | tf_op jit(solution)/shard_map/ppermute | solution.py:326
  13.1 25.4 %all-to-all-start = ((bf16[16,72,128]{2,1,0:T(8,128)(2,1)}), bf16[16,72,128]{2,1,0:T(8,128)(2,1)S(1)}, u32[]{:S(2)}, u32[]{:S(2)}) async-start(bf16[16,72,128]{2,1,0:T(8,128)(2,1)} %fusion), calls=%async_computation | async-start | bytes 589824 | tf_op jit(solution)/shard_map/all_to_all | solution.py:330

commit v2 on v1

--- a/solution.py
+++ b/solution.py
@@ -4,11 +4,14 @@
 from jax import lax
 from jax.experimental import pallas as pl
 from jax.experimental.pallas import tpu as pltpu
-from jax.sharding import PartitionSpec as P
+from jax.sharding import Mesh, PartitionSpec as P
 
 EPSILON = 1e-05
 PAIR = 128
-VMEM_BYTES = 58 * 1024 * 1024
+AXES = ("z", "xlo", "xhi", "y", "core")
+OUTER = ("z", "xlo")
+INNER = ("xhi", "y")
+VMEM_BYTES = 32 * 1024 * 1024
 BF16 = jnp.bfloat16
 F32 = jnp.float32
 
@@ -54,7 +57,7 @@
 
 def attend(
     wet_ref, bias_ref, x_ref, qkv_ref, mixed_ref, attended_ref, probs_ref, probs_low_ref, scores_ref, bias_t_ref,
-    normed_ref, inverse_ref, x_wait, small_waits, qkv_wait, sizes,
+    normed_ref, inverse_ref, x_wait, small_waits, qkv_wait, sizes, between=None,
 ):
     windows, cells, heads = sizes
     hidden = attended_ref.shape[1]
@@ -64,25 +67,30 @@
     spread, own = make_spread(cells, size)
 
     x_wait()
-    x_float = x_ref[...].astype(F32)
-    centred = x_float - jnp.mean(x_float, -1, keepdims=True)
-    inverse = lax.rsqrt(jnp.mean(centred * centred, -1, keepdims=True) + EPSILON)
-    normed = centred * inverse
-    if normed_ref is not None:
-        normed_ref[...] = normed
-        inverse_ref[...] = inverse
-    normed_low = normed.astype(BF16)
     small_waits()
     bias_t_ref[...] = bias_ref[...].T
     closed = jnp.where(wet_ref[...] > 0, 0.0, -jnp.inf).astype(F32).T
+    step = x_ref.shape[0] // 2
+    lows = []
+    for part in range(2):
+        at = slice(part * step, (part + 1) * step)
+        x_float = x_ref[at, :].astype(F32)
+        centred = x_float - jnp.mean(x_float, -1, keepdims=True)
+        inverse = lax.rsqrt(jnp.mean(centred * centred, -1, keepdims=True) + EPSILON)
+        normed = centred * inverse
+        if normed_ref is not None:
+            normed_ref[at, :] = normed
+            inverse_ref[at, :] = inverse
+        lows.append(normed.astype(BF16))
     qkv_wait()
-    for part in range(3):
-        lanes = slice(part * hidden, (part + 1) * hidden)
-        mixed = dot(normed_low, qkv_ref[:, lanes], 1, 0)
-        if part == 0:
-            mixed = mixed * scale
-        mixed_ref[:, lanes] = mixed.astype(BF16)
-
+    for part in range(2):
+        at = slice(part * step, (part + 1) * step)
+        mixed = dot(lows[part], qkv_ref[...], 1, 0)
+        mixed_ref[at, :hidden] = (mixed[:, :hidden] * scale).astype(BF16)
+        mixed_ref[at, hidden:] = mixed[:, hidden:].astype(BF16)
+
+    if between is not None:
+        between()
     for window in range(windows):
         at = slice(window * cells, (window + 1) * cells)
         for pair in range(pairs):
@@ -108,9 +116,9 @@
 
 
 def share_kernel(
-    wet_hbm, bias_hbm, count_ref, x_hbm, g_hbm, qkv_hbm, share_ref,
+    wet_hbm, bias_hbm, count_ref, x_hbm, g_hbm, qkv_hbm, held_ref, sent_ref,
     wet_ref, bias_ref, x_ref, g_ref, qkv_ref, mixed_ref, attended_ref, bias_t_ref, probs_low_ref, scores_ref,
-    lines_ref, sems, *, sizes, outer, inner,
+    turned_ref, lines_ref, sems, *, sizes, outer, inner,
 ):
     rows, width = x_ref.shape
     cells = sizes[1]
@@ -126,20 +134,28 @@
         bias_copy.wait()
         wet_copy.wait()
 
+    def turn():
+        g_copy.wait()
+        keep_live(g_ref, count_ref, cells)
+        turned_ref[...] = g_ref[...].T
+
     attend(
         wet_ref, bias_ref, x_ref, qkv_ref, mixed_ref, attended_ref, None, probs_low_ref, scores_ref, bias_t_ref,
-        None, None, x_copy.wait, small_waits, qkv_copy.wait, sizes,
-    )
-    g_copy.wait()
-    keep_live(g_ref, count_ref, cells)
-    total = dot(g_ref[...], attended_ref[...], 0, 0)
+        None, None, x_copy.wait, small_waits, qkv_copy.wait, sizes, turn,
+    )
+    total = dot(turned_ref[...], attended_ref[...], 1, 0)
+    half = width // 2
     for k in range(pairs):
-        part = total[:, k * PAIR : (k + 1) * PAIR].reshape(outer, inner, PAIR)
-        part = jnp.transpose(part, (1, 0, 2)).reshape(inner // 2, 2, outer, PAIR)
+        part = total[:, k * PAIR : (k + 1) * PAIR].reshape(outer, 2 * inner, PAIR)
+        part = jnp.transpose(part, (1, 0, 2)).reshape(inner, 2, outer, PAIR)
         for core in range(2):
-            lines = pl.ds(core * width * pairs // 2 + k, width // 2, stride=pairs)
-            lines_ref[lines, :] = part[:, core].reshape(width // 2, PAIR)
-    share_ref[...] = lines_ref[...].astype(BF16).reshape(share_ref.shape)
+            lines = pl.ds(core * half * pairs + k, half, stride=pairs)
+            lines_ref[lines, :] = part[:, core].reshape(half, PAIR)
+    core = lax.axis_index("core")
+    held = pl.ds(pl.multiple_of(core * half * pairs, half * pairs), half * pairs)
+    sent = pl.ds(pl.multiple_of((1 - core) * half * pairs, half * pairs), half * pairs)
+    held_ref[...] = lines_ref[held, :].astype(held_ref.dtype).reshape(held_ref.shape)
+    sent_ref[...] = lines_ref[sent, :].astype(sent_ref.dtype).reshape(sent_ref.shape)
 
 
 def grads_kernel(
@@ -253,6 +269,13 @@
     return specs[:2] + [pl.BlockSpec(memory_space=pltpu.SMEM)] + specs[2:]
 
 
+def pinned(args):
+    return [
+        arg if arg.size == 1 else pltpu.with_memory_space_constraint(arg, pltpu.HBM)
+        for arg in args
+    ]
+
+
 def share_call(x, g, wet, count, qkv_weight, score_bias, outer, inner):
     args, staged, worked, sizes = staging(x, g, wet, count, qkv_weight, score_bias)
     rows, width = args[3].shape
@@ -260,12 +283,16 @@
     pairs = hidden // PAIR
     return pl.pallas_call(
         functools.partial(share_kernel, sizes=sizes, outer=outer, inner=inner),
-        out_shape=jax.ShapeDtypeStruct((2, inner // 2, outer * pairs, PAIR), BF16),
+        out_shape=(
+            pltpu.VMEM((inner, outer * pairs, PAIR), F32),
+            pltpu.VMEM((inner, outer * pairs, PAIR), BF16),
+        ),
         in_specs=placed(5),
-        out_specs=pl.BlockSpec(memory_space=pltpu.VMEM),
+        out_specs=[pl.BlockSpec(memory_space=pltpu.VMEM)] * 2,
         scratch_shapes=staged
         + worked
         + [
+            pltpu.VMEM((width, rows), BF16),
             pltpu.VMEM((width * pairs, PAIR), F32),
             pltpu.SemaphoreType.DMA((5,)),
         ],
@@ -273,7 +300,7 @@
         cost_estimate=pl.CostEstimate(
             flops=2 * rows * width * 4 * hidden, bytes_accessed=4_000_000, transcendentals=200_000
         ),
-    )(*args)
+    )(*pinned(args))
 
 
 def grads_call(x, g, wet, count, qkv_weight, proj_weight, score_bias):
@@ -304,7 +331,7 @@
         cost_estimate=pl.CostEstimate(
             flops=2 * rows * width * 16 * hidden, bytes_accessed=30_000_000, transcendentals=200_000
         ),
-    )(*args, proj_weight)
+    )(*pinned(args + (proj_weight,)))
 
 
 def block_call(x, g, wet, count, qkv_weight, proj_weight, score_bias, outer, inner):
@@ -313,38 +340,35 @@
     return out, grad, share
 
 
-def shards(windows_in, cotangent, wet_mask, wet_count, qkv_weight, proj_weight, score_bias):
-    outer, inner = lax.axis_size("space"), lax.axis_size("dp")
+def shards(windows_in, cotangent, wet, count, qkv_weight, proj_weight, score_bias):
+    outer, inner = lax.axis_size(OUTER), lax.axis_size(INNER)
     pairs = proj_weight.shape[1] // PAIR
-    x, g = windows_in[0], cotangent[0]
-    wet, count = wet_mask[0], wet_count
-    share = share_call(x, g, wet, count, qkv_weight, score_bias, outer, inner)
-    pairs_of_cores = [(i, i ^ 1) for i in range(inner)]
-    core = lax.rem(lax.axis_index("dp"), 2)
-    sent = lax.dynamic_index_in_dim(share, 1 - core, 0, keepdims=False)
-    held = lax.dynamic_index_in_dim(share, core, 0, keepdims=False)
-    got = lax.ppermute(sent, "dp", pairs_of_cores)
-    share = (held.astype(F32) + got.astype(F32)).astype(BF16)
+    x, g, wet = windows_in[0], cotangent[0], wet[0]
+    held, sent = share_call(x, g, wet, count, qkv_weight, score_bias, outer, inner)
+    got = lax.ppermute(sent, "core", [(0, 1), (1, 0)])
+    share = (held + got.astype(F32)).astype(BF16)
     wet, share = lax.optimization_barrier((wet, share))
-    groups = [list(range(core, inner, 2)) for core in range(2)]
-    got = lax.all_to_all(share, "dp", 0, 0, tiled=True, axis_index_groups=groups)
+    got = lax.all_to_all(share, INNER, 0, 0, tiled=True)
     out, grad = grads_call(x, g, wet, count, qkv_weight, proj_weight, score_bias)
     got, out, grad = lax.optimization_barrier((got, out, grad))
-    part = jnp.sum(got.astype(F32), 0).astype(BF16).reshape(outer, pairs, PAIR)
-    got = lax.all_to_all(part, "space", 0, 0, tiled=True)
-    total = jnp.sum(got.astype(F32), 0).reshape(-1)
+    part = jnp.sum(got.astype(F32), 0).reshape(outer, pairs, PAIR)
+    got = lax.all_to_all(part, OUTER, 0, 0, tiled=True)
+    total = jnp.sum(got, 0).reshape(-1)
     return (out.reshape(windows_in.shape), grad.reshape(windows_in.shape), total)
 
 
 def solution(mesh):
+    space, dp = mesh.devices.shape
+    split = Mesh(mesh.devices.reshape(space // 2, 2, 2, dp // 4, 2), AXES)
+    tiles, samples = ("z", "xlo"), ("xhi", "y", "core")
     in_specs = (
-        P("dp", "space", None, None),
-        P("dp", "space", None, None),
-        P("dp", "space", None),
-        P("dp", "space"),
+        P(samples, tiles, None, None),
+        P(samples, tiles, None, None),
+        P(samples, tiles, None),
+        P(samples, tiles),
         P(),
         P(),
         P(),
     )
-    out_specs = (P("dp", "space", None, None), P("dp", "space", None, None), P(("space", "dp")))
-    return jax.shard_map(shards, mesh=mesh, in_specs=in_specs, out_specs=out_specs, check_vma=False)
+    out_specs = (P(samples, tiles, None, None), P(samples, tiles, None, None), P(AXES))
+    return jax.shard_map(shards, mesh=split, in_specs=in_specs, out_specs=out_specs, check_vma=False)

time: 62.7 us -> 59.7 us (0.952)
  Pallas kernels: 14.7 us -> 13.6 us
  local copies, waits for them, and re-layouts: 1.01 us -> 0.02 us
  other arithmetic: 2.41 us -> 1.43 us
    pallas_call x1, Pallas kernels: 5.58 us -> 4.57 us  [share_call(): pl.pallas_call(functools.partial(share_kernel, sizes=sizes, outer=outer,...]
    squeeze x1 -> x0, local copies, waits for them, and re-layouts: 0.99 us -> none  [shards(): sent = lax.dynamic_index_in_dim(share, 1 - core, 0, keepdims=False)]
    convert_element_type x1, other arithmetic: 1.75 us -> 0.78 us  [shards(): share = (held + got.astype(F32)).astype(BF16)]
where the time goes in v2:
time: 59.7 us; the launch traced here: 59.4 us
  blocking collectives  23.2 us (39%)
  starting transfers between devices  14.7 us (25%)
  Pallas kernels  13.6 us (23%)
  waiting for transfers between devices  5.13 us (9%)
  other arithmetic  1.43 us (2%)
  between operations  1.31 us (2%)
    all_to_all x1, blocking collectives, shards(): got = lax.all_to_all(part, OUTER, 0, 0, tiled=True)  23.2 us
    all_to_all x1, starting transfers between devices, shards(): got = lax.all_to_all(share, INNER, 0, 0, tiled=True)  12.8 us
    pallas_call x1, Pallas kernels, grads_call(): pl.pallas_call(functools.partial(grads_kernel, sizes=sizes), out_shape=(f...  8.99 us
    pallas_call x1, Pallas kernels, share_call(): pl.pallas_call(functools.partial(share_kernel, sizes=sizes, outer=outer,...  4.57 us
    all_to_all x1, waiting for transfers between devices, shards(): got = lax.all_to_all(share, INNER, 0, 0, tiled=True)  3.59 us
    ppermute x1, starting transfers between devices, shards(): got = lax.ppermute(sent, 'core', [(0, 1), (1, 0)])  1.92 us
    ppermute x1, waiting for transfers between devices, shards(): got = lax.ppermute(sent, 'core', [(0, 1), (1, 0)])  1.55 us
  transfers between devices with their start and end apart: 2, of which 2 were waited for; matrix products, arithmetic and copies ran while one was open for 0% of the time, Pallas kernels for 15%

profile of v2, /device:TPU:8, one launch (start us, length us, event | category | flops | bytes accessed | tf_op | source)
XLA Modules:
  0.0 59.4 jit_solution(13490581734406931853)
XLA Ops:
  1.3 4.6 %shard_map.94 = (f32[16,72,128]{2,1,0:T(8,128)S(1)}, bf16[16,72,128]{2,1,0:T(8,128)(2,1)S(1)}) custom-call(s32[8,64]{1,0:T(8,128)} %bitcast.14, f32[384,64]{1,0:T(8,128)} %bitcast.12, s32[1,1]{1,0:T(1,128)S(6)} %copy.10.count_ref, bf16[512,768]{1,0:T(8,128)(2,1)} %bitcast.8, bf16[512,768]{1,0:T(8,128)(2,1)} %bitcast.10, bf16[768,1152]{1,0:T(8,128)(2,1)} %qkv_hbm.3), custom_call_target="tpu_custom_call" | custom-call | flops 1207959552 | bytes 4000000 | tf_op jit(solution)/shard_map/pallas_call | solution.py:284
  5.9 1.9 %collective-permute-start = (bf16[16,72,128]{2,1,0:T(8,128)(2,1)S(1)}, bf16[16,72,128]{2,1,0:T(8,128)(2,1)S(1)}, u32[]{:S(2)}, u32[]{:S(2)}) collective-permute-start(bf16[16,72,128]{2,1,0:T(8,128)(2,1)S(1)} %get-tuple-element.13), channel_id=1, source_target_pairs={{0,1},{1,0},{2,3},{3,2},{4,5},{5,4},{6,7},{7,6},{8,9},{9,8},{10,11... | collective-permute-start | bytes 884744 | tf_op jit(solution)/shard_map/ppermute | solution.py:348
  7.8 1.5 %collective-permute-done = bf16[16,72,128]{2,1,0:T(8,128)(2,1)S(1)} collective-permute-done((bf16[16,72,128]{2,1,0:T(8,128)(2,1)S(1)}, bf16[16,72,128]{2,1,0:T(8,128)(2,1)S(1)}, u32[]{:S(2)}, u32[]{:S(2)}) %collective-permute-start) | collective-permute-done | bytes 294944 | tf_op jit(solution)/shard_map/ppermute | solution.py:348
  9.3 0.8 %add_convert_fusion = bf16[16,72,128]{2,1,0:T(8,128)(2,1)} fusion(f32[16,72,128]{2,1,0:T(8,128)S(1)} %get-tuple-element.12, bf16[16,72,128]{2,1,0:T(8,128)(2,1)S(1)} %collective-permute-done), kind=kLoop, calls=%fused_computation.1 | loop fusion | flops 442368 | bytes 1179648 | tf_op jit(solution)/shard_map/convert_element_type | solution.py:349
  10.1 12.8 %all-to-all-start = ((bf16[16,72,128]{2,1,0:T(8,128)(2,1)}), bf16[16,72,128]{2,1,0:T(8,128)(2,1)S(1)}, u32[]{:S(2)}, u32[]{:S(2)}) async-start(bf16[16,72,128]{2,1,0:T(8,128)(2,1)} %add_convert_fusion), calls=%async_computation | async-start | bytes 589824 | tf_op jit(solution)/shard_map/all_to_all | solution.py:351
  22.9 9.0 %shard_map.95 = (bf16[512,768]{1,0:T(8,128)(2,1)}, bf16[512,768]{1,0:T(8,128)(2,1)}) custom-call(s32[8,64]{1,0:T(8,128)} %bitcast.15, f32[384,64]{1,0:T(8,128)} %bitcast.13, s32[1,1]{1,0:T(1,128)S(6)} %copy.10.count_ref, bf16[512,768]{1,0:T(8,128)(2,1)} %bitcast.9, bf16[512,768]{1,0:T(8,128)(2,1)} %bitcast.11, bf16[768,1152]{1,0:T(8,128)(2,1)} %qkv_hbm.3, ...), custom_call_target="tpu_custom_call" | custom-call | flops 4831838208 | bytes 30000000 | tf_op jit(solution)/shard_map/pallas_call | solution.py:312
  31.9 3.6 %all-to-all-done = bf16[16,72,128]{2,1,0:T(8,128)(2,1)S(1)} async-done(((bf16[16,72,128]{2,1,0:T(8,128)(2,1)}), bf16[16,72,128]{2,1,0:T(8,128)(2,1)S(1)}, u32[]{:S(2)}, u32[]{:S(2)}) %all-to-all-start) | async-done | bytes 294944 | tf_op jit(solution)/shard_map/all_to_all | solution.py:351
  35.6 23.2 %all_to_all.10 = f32[24,3,128]{2,1,0:T(4,128)S(1)} all-to-all(f32[24,3,128]{2,1,0:T(4,128)S(1)} %reshape.25), channel_id=1, replica_groups=mesh['z'=12,'xlo'=2,'xhi'=2,'y'=8,'core'=2] {'z','xlo'}, dimensions={0} | all-to-all | bytes 73728 | tf_op jit(solution)/shard_map/all_to_all | solution.py:355
  58.8 0.6 %reduce_sum.19 = f32[3,128]{1,0:T(4,128)} reduce(f32[24,3,128]{2,1,0:T(4,128)S(1)} %all_to_all.10, f32[]{:T(128)} %constant.0.clone.1), dimensions={0}, to_apply=%region_1.0 | reduce | flops 8832 | bytes 38404 | tf_op jit(solution)/shard_map/reduce_sum | solution.py:356
  (2 shorter events, 0.1 us)
Async XLA Ops:
  5.9 3.5 %collective-permute-start = (bf16[16,72,128]{2,1,0:T(8,128)(2,1)S(1)}, bf16[16,72,128]{2,1,0:T(8,128)(2,1)S(1)}, u32[]{:S(2)}, u32[]{:S(2)}) collective-permute-start(bf16[16,72,128]{2,1,0:T(8,128)(2,1)S(1)} %get-tuple-element.13), channel_id=1, source_target_pairs={{0,1},{1,0},{2,3},{3,2},{4,5},{5,4},{6,7},{7,6},{8,9},{9,8},{10,11... | collective-permute-start | bytes 884744 | tf_op jit(solution)/shard_map/ppermute | solution.py:348
  10.1 25.4 %all-to-all-start = ((bf16[16,72,128]{2,1,0:T(8,128)(2,1)}), bf16[16,72,128]{2,1,0:T(8,128)(2,1)S(1)}, u32[]{:S(2)}, u32[]{:S(2)}) async-start(bf16[16,72,128]{2,1,0:T(8,128)(2,1)} %add_convert_fusion), calls=%async_computation | async-start | bytes 589824 | tf_op jit(solution)/shard_map/all_to_all | solution.py:351

commit v3 on v2

--- a/solution.py
+++ b/solution.py
@@ -4,13 +4,12 @@
 from jax import lax
 from jax.experimental import pallas as pl
 from jax.experimental.pallas import tpu as pltpu
-from jax.sharding import Mesh, PartitionSpec as P
+from jax.sharding import PartitionSpec as P
 
 EPSILON = 1e-05
 PAIR = 128
-AXES = ("z", "xlo", "xhi", "y", "core")
-OUTER = ("z", "xlo")
-INNER = ("xhi", "y")
+FIRST_OUTER = 19
+FIRST_INNER = 13
 VMEM_BYTES = 32 * 1024 * 1024
 BF16 = jnp.bfloat16
 F32 = jnp.float32
@@ -36,6 +35,10 @@
         return jnp.where(first_head, both[:cells], both[cells:])
 
     return spread, own
+
+
+def turned_by(array, first):
+    return jnp.concatenate([array[first:], array[:first]], 0)
 
 
 def keep_live(ref, count_ref, cells):
@@ -147,11 +150,13 @@
     half = width // 2
     for k in range(pairs):
         part = total[:, k * PAIR : (k + 1) * PAIR].reshape(outer, 2 * inner, PAIR)
+        part = turned_by(part, FIRST_OUTER)
         part = jnp.transpose(part, (1, 0, 2)).reshape(inner, 2, outer, PAIR)
+        part = turned_by(part, FIRST_INNER)
         for core in range(2):
             lines = pl.ds(core * half * pairs + k, half, stride=pairs)
             lines_ref[lines, :] = part[:, core].reshape(half, PAIR)
-    core = lax.axis_index("core")
+    core = lax.rem(lax.axis_index("dp"), 2)
     held = pl.ds(pl.multiple_of(core * half * pairs, half * pairs), half * pairs)
     sent = pl.ds(pl.multiple_of((1 - core) * half * pairs, half * pairs), half * pairs)
     held_ref[...] = lines_ref[held, :].astype(held_ref.dtype).reshape(held_ref.shape)
@@ -293,7 +298,7 @@
         + worked
         + [
             pltpu.VMEM((width, rows), BF16),
-            pltpu.VMEM((width * pairs, PAIR), F32),
+            pltpu.VMEM((width * pairs + 8, PAIR), F32),
             pltpu.SemaphoreType.DMA((5,)),
         ],
         compiler_params=pltpu.CompilerParams(vmem_limit_bytes=VMEM_BYTES),
@@ -334,41 +339,35 @@
     )(*pinned(args + (proj_weight,)))
 
 
-def block_call(x, g, wet, count, qkv_weight, proj_weight, score_bias, outer, inner):
-    share = share_call(x, g, wet, count, qkv_weight, score_bias, outer, inner)
-    out, grad = grads_call(x, g, wet, count, qkv_weight, proj_weight, score_bias)
-    return out, grad, share
-
-
 def shards(windows_in, cotangent, wet, count, qkv_weight, proj_weight, score_bias):
-    outer, inner = lax.axis_size(OUTER), lax.axis_size(INNER)
+    outer, samples = lax.axis_size("space"), lax.axis_size("dp")
+    inner = samples // 2
     pairs = proj_weight.shape[1] // PAIR
     x, g, wet = windows_in[0], cotangent[0], wet[0]
     held, sent = share_call(x, g, wet, count, qkv_weight, score_bias, outer, inner)
-    got = lax.ppermute(sent, "core", [(0, 1), (1, 0)])
+    got = lax.ppermute(sent, "dp", [(i, i ^ 1) for i in range(samples)])
     share = (held + got.astype(F32)).astype(BF16)
     wet, share = lax.optimization_barrier((wet, share))
-    got = lax.all_to_all(share, INNER, 0, 0, tiled=True)
+    groups = [[2 * ((j + FIRST_INNER) % inner) + core for j in range(inner)] for core in range(2)]
+    got = lax.all_to_all(share, "dp", 0, 0, tiled=True, axis_index_groups=groups)
     out, grad = grads_call(x, g, wet, count, qkv_weight, proj_weight, score_bias)
     got, out, grad = lax.optimization_barrier((got, out, grad))
     part = jnp.sum(got.astype(F32), 0).reshape(outer, pairs, PAIR)
-    got = lax.all_to_all(part, OUTER, 0, 0, tiled=True)
+    groups = [[(j + FIRST_OUTER) % outer for j in range(outer)]]
+    got = lax.all_to_all(part, "space", 0, 0, tiled=True, axis_index_groups=groups)
     total = jnp.sum(got, 0).reshape(-1)
     return (out.reshape(windows_in.shape), grad.reshape(windows_in.shape), total)
 
 
 def solution(mesh):
-    space, dp = mesh.devices.shape
-    split = Mesh(mesh.devices.reshape(space // 2, 2, 2, dp // 4, 2), AXES)
-    tiles, samples = ("z", "xlo"), ("xhi", "y", "core")
     in_specs = (
-        P(samples, tiles, None, None),
-        P(samples, tiles, None, None),
-        P(samples, tiles, None),
-        P(samples, tiles),
+        P("dp", "space", None, None),
+        P("dp", "space", None, None),
+        P("dp", "space", None),
+        P("dp", "space"),
         P(),
         P(),
         P(),
     )
-    out_specs = (P(samples, tiles, None, None), P(samples, tiles, None, None), P(AXES))
-    return jax.shard_map(shards, mesh=split, in_specs=in_specs, out_specs=out_specs, check_vma=False)
+    out_specs = (P("dp", "space", None, None), P("dp", "space", None, None), P(("space", "dp")))
+    return jax.shard_map(shards, mesh=mesh, in_specs=in_specs, out_specs=out_specs, check_vma=False)

time: 59.7 us -> 54.4 us (0.911)
  the two profiles are of different devices: /device:TPU:8 before, /device:TPU:2 now
where the time goes in v3:
time: 54.4 us; the launch traced here: 54.1 us
  blocking collectives  24.2 us (44%)
  Pallas kernels  13.6 us (25%)
  starting transfers between devices  12 us (22%)
  waiting for transfers between devices  1.55 us (3%)
  other arithmetic  1.44 us (3%)
  between operations  1.32 us (2%)
    all_to_all x1, blocking collectives, shards(): lax.all_to_all(part, 'space', 0, 0, tiled=True, axis_index_groups=groups)  24.2 us
    all_to_all x1, starting transfers between devices, shards(): lax.all_to_all(share, 'dp', 0, 0, tiled=True, axis_index_groups=groups)  10.1 us
    pallas_call x1, Pallas kernels, grads_call(): pl.pallas_call(functools.partial(grads_kernel, sizes=sizes), out_shape=(f...  8.99 us
    pallas_call x1, Pallas kernels, share_call(): pl.pallas_call(functools.partial(share_kernel, sizes=sizes, outer=outer,...  4.6 us
    ppermute x1, starting transfers between devices, shards(): got = lax.ppermute(sent, 'dp', [(i, i ^ 1) for i in range(samples)])  1.92 us
    ppermute x1, waiting for transfers between devices, shards(): got = lax.ppermute(sent, 'dp', [(i, i ^ 1) for i in range(samples)])  1.55 us
  transfers between devices with their start and end apart: 2, of which 1 were waited for; matrix products, arithmetic and copies ran while one was open for 0% of the time, Pallas kernels for 17%

profile of v3, /device:TPU:2, one launch (start us, length us, event | category | flops | bytes accessed | tf_op | source)
XLA Modules:
  0.0 54.1 jit_solution(15804134695186770920)
XLA Ops:
  1.3 4.6 %shard_map.94 = (f32[16,72,128]{2,1,0:T(8,128)S(1)}, bf16[16,72,128]{2,1,0:T(8,128)(2,1)S(1)}) custom-call(s32[8,64]{1,0:T(8,128)} %bitcast.14, f32[384,64]{1,0:T(8,128)} %bitcast.12, s32[1,1]{1,0:T(1,128)S(6)} %copy.10.count_ref, bf16[512,768]{1,0:T(8,128)(2,1)} %bitcast.8, bf16[512,768]{1,0:T(8,128)(2,1)} %bitcast.10, bf16[768,1152]{1,0:T(8,128)(2,1)} %qkv_hbm.3), custom_call_target="tpu_custom_call" | custom-call | flops 1207959552 | bytes 4000000 | tf_op jit(solution)/shard_map/pallas_call | solution.py:289
  5.9 1.9 %collective-permute-start = (bf16[16,72,128]{2,1,0:T(8,128)(2,1)S(1)}, bf16[16,72,128]{2,1,0:T(8,128)(2,1)S(1)}, u32[]{:S(2)}, u32[]{:S(2)}) collective-permute-start(bf16[16,72,128]{2,1,0:T(8,128)(2,1)S(1)} %get-tuple-element.13), channel_id=1, source_target_pairs={{0,1},{1,0},{2,3},{3,2},{4,5},{5,4},{6,7},{7,6},{8,9},{9,8},{10,11... | collective-permute-start | bytes 884744 | tf_op jit(solution)/shard_map/ppermute | solution.py:348
  7.8 1.5 %collective-permute-done = bf16[16,72,128]{2,1,0:T(8,128)(2,1)S(1)} collective-permute-done((bf16[16,72,128]{2,1,0:T(8,128)(2,1)S(1)}, bf16[16,72,128]{2,1,0:T(8,128)(2,1)S(1)}, u32[]{:S(2)}, u32[]{:S(2)}) %collective-permute-start) | collective-permute-done | bytes 294944 | tf_op jit(solution)/shard_map/ppermute | solution.py:348
  9.4 0.8 %add_convert_fusion = bf16[16,72,128]{2,1,0:T(8,128)(2,1)} fusion(f32[16,72,128]{2,1,0:T(8,128)S(1)} %get-tuple-element.12, bf16[16,72,128]{2,1,0:T(8,128)(2,1)S(1)} %collective-permute-done), kind=kLoop, calls=%fused_computation.1 | loop fusion | flops 442368 | bytes 1179648 | tf_op jit(solution)/shard_map/convert_element_type | solution.py:349
  10.1 10.1 %all-to-all-start = ((bf16[16,72,128]{2,1,0:T(8,128)(2,1)}), bf16[16,72,128]{2,1,0:T(8,128)(2,1)S(1)}, u32[]{:S(2)}, u32[]{:S(2)}) async-start(bf16[16,72,128]{2,1,0:T(8,128)(2,1)} %add_convert_fusion), calls=%async_computation | async-start | bytes 589824 | tf_op jit(solution)/shard_map/all_to_all | solution.py:352
  20.2 9.0 %shard_map.95 = (bf16[512,768]{1,0:T(8,128)(2,1)}, bf16[512,768]{1,0:T(8,128)(2,1)}) custom-call(s32[8,64]{1,0:T(8,128)} %bitcast.15, f32[384,64]{1,0:T(8,128)} %bitcast.13, s32[1,1]{1,0:T(1,128)S(6)} %copy.10.count_ref, bf16[512,768]{1,0:T(8,128)(2,1)} %bitcast.9, bf16[512,768]{1,0:T(8,128)(2,1)} %bitcast.11, bf16[768,1152]{1,0:T(8,128)(2,1)} %qkv_hbm.3, ...), custom_call_target="tpu_custom_call" | custom-call | flops 4831838208 | bytes 30000000 | tf_op jit(solution)/shard_map/pallas_call | solution.py:317
  29.2 0.0 all-to-all-done
  29.3 24.2 %all_to_all.10 = f32[24,3,128]{2,1,0:T(4,128)S(1)} all-to-all(f32[24,3,128]{2,1,0:T(4,128)S(1)} %reshape.25), channel_id=1, replica_groups={{608,640,672,704,736,0,32,64,96,128,160,192,224,256,288,320,352,384,416..., dimensions={0} | all-to-all | bytes 73728 | tf_op jit(solution)/shard_map/all_to_all | solution.py:357
  53.5 0.6 %reduce_sum.19 = f32[3,128]{1,0:T(4,128)} reduce(f32[24,3,128]{2,1,0:T(4,128)S(1)} %all_to_all.10, f32[]{:T(128)} %constant.0.clone.1), dimensions={0}, to_apply=%region_1.0 | reduce | flops 8832 | bytes 38404 | tf_op jit(solution)/shard_map/reduce_sum | solution.py:358
  (2 shorter events, 0.1 us)
Async XLA Ops:
  5.9 3.5 %collective-permute-start = (bf16[16,72,128]{2,1,0:T(8,128)(2,1)S(1)}, bf16[16,72,128]{2,1,0:T(8,128)(2,1)S(1)}, u32[]{:S(2)}, u32[]{:S(2)}) collective-permute-start(bf16[16,72,128]{2,1,0:T(8,128)(2,1)S(1)} %get-tuple-element.13), channel_id=1, source_target_pairs={{0,1},{1,0},{2,3},{3,2},{4,5},{5,4},{6,7},{7,6},{8,9},{9,8},{10,11... | collective-permute-start | bytes 884744 | tf_op jit(solution)/shard_map/ppermute | solution.py:348
  10.1 19.1 %all-to-all-start = ((bf16[16,72,128]{2,1,0:T(8,128)(2,1)}), bf16[16,72,128]{2,1,0:T(8,128)(2,1)S(1)}, u32[]{:S(2)}, u32[]{:S(2)}) async-start(bf16[16,72,128]{2,1,0:T(8,128)(2,1)} %add_convert_fusion), calls=%async_computation | async-start | bytes 589824 | tf_op jit(solution)/shard_map/all_to_all | solution.py:352

commit v4 on v3

--- a/solution.py
+++ b/solution.py
@@ -8,8 +8,10 @@
 
 EPSILON = 1e-05
 PAIR = 128
-FIRST_OUTER = 19
-FIRST_INNER = 13
+CORE_COLUMNS = ((1, 1), (0, 1), (1, 0), (0, 0))
+COLUMNS = tuple((*column, core, odd) for core in (1, 0) for column in CORE_COLUMNS for odd in (1, 0))
+FIRST_Z = 4
+FIRST_Y = 4
 VMEM_BYTES = 32 * 1024 * 1024
 BF16 = jnp.bfloat16
 F32 = jnp.float32
@@ -37,8 +39,9 @@
     return spread, own
 
 
-def turned_by(array, first):
-    return jnp.concatenate([array[first:], array[:first]], 0)
+def turned_by(array, first, axis):
+    before, after = jnp.split(array, [first], axis)
+    return jnp.concatenate([after, before], axis)
 
 
 def keep_live(ref, count_ref, cells):
@@ -119,9 +122,9 @@
 
 
 def share_kernel(
-    wet_hbm, bias_hbm, count_ref, x_hbm, g_hbm, qkv_hbm, held_ref, sent_ref,
+    wet_hbm, bias_hbm, count_ref, x_hbm, g_hbm, qkv_hbm, share_hbm,
     wet_ref, bias_ref, x_ref, g_ref, qkv_ref, mixed_ref, attended_ref, bias_t_ref, probs_low_ref, scores_ref,
-    turned_ref, lines_ref, sems, *, sizes, outer, inner,
+    turned_ref, total_ref, lines_ref, share_ref, sems, *, sizes, zs, ys,
 ):
     rows, width = x_ref.shape
     cells = sizes[1]
@@ -147,20 +150,26 @@
         None, None, x_copy.wait, small_waits, qkv_copy.wait, sizes, turn,
     )
     total = dot(turned_ref[...], attended_ref[...], 1, 0)
-    half = width // 2
     for k in range(pairs):
-        part = total[:, k * PAIR : (k + 1) * PAIR].reshape(outer, 2 * inner, PAIR)
-        part = turned_by(part, FIRST_OUTER)
-        part = jnp.transpose(part, (1, 0, 2)).reshape(inner, 2, outer, PAIR)
-        part = turned_by(part, FIRST_INNER)
-        for core in range(2):
-            lines = pl.ds(core * half * pairs + k, half, stride=pairs)
-            lines_ref[lines, :] = part[:, core].reshape(half, PAIR)
-    core = lax.rem(lax.axis_index("dp"), 2)
-    held = pl.ds(pl.multiple_of(core * half * pairs, half * pairs), half * pairs)
-    sent = pl.ds(pl.multiple_of((1 - core) * half * pairs, half * pairs), half * pairs)
-    held_ref[...] = lines_ref[held, :].astype(held_ref.dtype).reshape(held_ref.shape)
-    sent_ref[...] = lines_ref[sent, :].astype(sent_ref.dtype).reshape(sent_ref.shape)
+        total_ref[k, :width, :] = total[:, k * PAIR : (k + 1) * PAIR]
+    lines = zs // 2 * ys * pairs
+    copies = []
+    for core in (1, 0):
+        for k in range(pairs):
+            part = total_ref[k, pl.ds(core, width // 2, stride=2), :].reshape(zs * 4, ys, PAIR)
+            part = turned_by(part, FIRST_Y, 1).reshape(zs // 2, 8, ys, PAIR)
+            part = turned_by(part, FIRST_Z, 0)
+            for column in range(8):
+                odd, xlo, xhi = column // 4, column // 2 % 2, column % 2
+                first = COLUMNS.index((xlo, xhi, core, odd)) * lines + k
+                lines_ref[pl.ds(first, lines // pairs, stride=pairs), :] = part[:, column].reshape(lines // pairs, PAIR)
+        first = 8 * (1 - core)
+        done = lines_ref[first * lines : (first + 8) * lines, :].astype(BF16)
+        share_ref[first : first + 8] = done.reshape(8, lines, PAIR)
+        at = slice(first, first + 8)
+        copies.append(fetch(share_ref.at[at], share_hbm.at[at]))
+    for copy in copies:
+        copy.wait()
 
 
 def grads_kernel(
@@ -281,25 +290,24 @@
     ]
 
 
-def share_call(x, g, wet, count, qkv_weight, score_bias, outer, inner):
+def share_call(x, g, wet, count, qkv_weight, score_bias, zs, ys):
     args, staged, worked, sizes = staging(x, g, wet, count, qkv_weight, score_bias)
     rows, width = args[3].shape
     hidden = qkv_weight.shape[1] // 3
     pairs = hidden // PAIR
     return pl.pallas_call(
-        functools.partial(share_kernel, sizes=sizes, outer=outer, inner=inner),
-        out_shape=(
-            pltpu.VMEM((inner, outer * pairs, PAIR), F32),
-            pltpu.VMEM((inner, outer * pairs, PAIR), BF16),
-        ),
+        functools.partial(share_kernel, sizes=sizes, zs=zs, ys=ys),
+        out_shape=pltpu.HBM((16, zs // 2 * ys * pairs, PAIR), BF16),
         in_specs=placed(5),
-        out_specs=[pl.BlockSpec(memory_space=pltpu.VMEM)] * 2,
+        out_specs=pl.BlockSpec(memory_space=pltpu.HBM),
         scratch_shapes=staged
         + worked
         + [
             pltpu.VMEM((width, rows), BF16),
+            pltpu.VMEM((pairs, width + 8, PAIR), F32),
             pltpu.VMEM((width * pairs + 8, PAIR), F32),
-            pltpu.SemaphoreType.DMA((5,)),
+            pltpu.VMEM((16, zs // 2 * ys * pairs, PAIR), BF16),
+            pltpu.SemaphoreType.DMA((7,)),
         ],
         compiler_params=pltpu.CompilerParams(vmem_limit_bytes=VMEM_BYTES),
         cost_estimate=pl.CostEstimate(
@@ -340,22 +348,27 @@
 
 
 def shards(windows_in, cotangent, wet, count, qkv_weight, proj_weight, score_bias):
-    outer, samples = lax.axis_size("space"), lax.axis_size("dp")
-    inner = samples // 2
+    zs, ys = lax.axis_size("space") // 2, lax.axis_size("dp") // 4
+    both = ("space", "dp")
     pairs = proj_weight.shape[1] // PAIR
     x, g, wet = windows_in[0], cotangent[0], wet[0]
-    held, sent = share_call(x, g, wet, count, qkv_weight, score_bias, outer, inner)
-    got = lax.ppermute(sent, "dp", [(i, i ^ 1) for i in range(samples)])
-    share = (held + got.astype(F32)).astype(BF16)
+
+    def device(half_z, y, column):
+        xlo, xhi, core, odd = column
+        return ((((2 * half_z + odd) * 2 + xlo) * 2 + xhi) * ys + y) * 2 + core
+
+    half = zs // 2
+    places = [((FIRST_Z + i) % half, (FIRST_Y + j) % ys) for i in range(half) for j in range(ys)]
+    near = [[device(*place, column) for column in COLUMNS] for place in places]
+    far = [[device(*place, column) for place in places] for column in COLUMNS]
+    share = share_call(x, g, wet, count, qkv_weight, score_bias, zs, ys)
     wet, share = lax.optimization_barrier((wet, share))
-    groups = [[2 * ((j + FIRST_INNER) % inner) + core for j in range(inner)] for core in range(2)]
-    got = lax.all_to_all(share, "dp", 0, 0, tiled=True, axis_index_groups=groups)
+    got = lax.all_to_all(share, both, 0, 0, tiled=True, axis_index_groups=near)
     out, grad = grads_call(x, g, wet, count, qkv_weight, proj_weight, score_bias)
     got, out, grad = lax.optimization_barrier((got, out, grad))
-    part = jnp.sum(got.astype(F32), 0).reshape(outer, pairs, PAIR)
-    groups = [[(j + FIRST_OUTER) % outer for j in range(outer)]]
-    got = lax.all_to_all(part, "space", 0, 0, tiled=True, axis_index_groups=groups)
-    total = jnp.sum(got, 0).reshape(-1)
+    part = jnp.sum(got.astype(F32), 0).astype(BF16).reshape(half * ys, pairs, PAIR)
+    got = lax.all_to_all(part, both, 0, 0, tiled=True, axis_index_groups=far)
+    total = jnp.sum(got.astype(F32), 0).reshape(-1)
     return (out.reshape(windows_in.shape), grad.reshape(windows_in.shape), total)
 
 

time: 54.4 us -> 50.7 us (0.932)
  the two profiles are of different devices: /device:TPU:2 before, /device:TPU:8 now
where the time goes in v4:
time: 50.7 us; the launch traced here: 50.5 us
  blocking collectives  26.5 us (52%)
  Pallas kernels  14.4 us (28%)
  starting transfers between devices  7.48 us (15%)
  between operations  1.31 us (3%)
  other arithmetic  0.72 us (1%)
    all_to_all x1, blocking collectives, shards(): got = lax.all_to_all(part, both, 0, 0, tiled=True, axis_index_groups=far)  26.5 us
    pallas_call x1, Pallas kernels, grads_call(): pl.pallas_call(functools.partial(grads_kernel, sizes=sizes), out_shape=(f...  8.98 us
    all_to_all x1, starting transfers between devices, shards(): got = lax.all_to_all(share, both, 0, 0, tiled=True, axis_index_groups=near)  7.48 us
    pallas_call x1, Pallas kernels, share_call(): pl.pallas_call(functools.partial(share_kernel, sizes=sizes, zs=zs, ys=ys)...  5.41 us
  transfers between devices with their start and end apart: 1, of which 0 were waited for; matrix products, arithmetic and copies ran while one was open for 0% of the time, Pallas kernels for 18%

profile of v4, /device:TPU:8, one launch (start us, length us, event | category | flops | bytes accessed | tf_op | source)
XLA Modules:
  0.0 50.5 jit_solution(8354448325564073556)
XLA Ops:
  1.3 5.4 %shard_map.94 = bf16[16,144,128]{2,1,0:T(8,128)(2,1)} custom-call(s32[8,64]{1,0:T(8,128)} %bitcast.14, f32[384,64]{1,0:T(8,128)} %bitcast.12, s32[1,1]{1,0:T(1,128)S(6)} %copy.10.count_ref, bf16[512,768]{1,0:T(8,128)(2,1)} %bitcast.8, bf16[512,768]{1,0:T(8,128)(2,1)} %bitcast.10, bf16[768,1152]{1,0:T(8,128)(2,1)} %qkv_hbm.3), custom_call_target="tpu_custom_call" | custom-call | flops 1207959552 | bytes 4000000 | tf_op jit(solution)/shard_map/pallas_call | solution.py:298
  6.7 7.5 %all-to-all-start = ((bf16[16,144,128]{2,1,0:T(8,128)(2,1)}), bf16[16,144,128]{2,1,0:T(8,128)(2,1)S(1)}, u32[]{:S(2)}, u32[]{:S(2)}) async-start(bf16[16,144,128]{2,1,0:T(8,128)(2,1)} %shard_map.94), calls=%async_computation | async-start | bytes 1179648 | tf_op jit(solution)/shard_map/all_to_all | solution.py:366
  14.2 9.0 %shard_map.95 = (bf16[512,768]{1,0:T(8,128)(2,1)}, bf16[512,768]{1,0:T(8,128)(2,1)}) custom-call(s32[8,64]{1,0:T(8,128)} %bitcast.15, f32[384,64]{1,0:T(8,128)} %bitcast.13, s32[1,1]{1,0:T(1,128)S(6)} %copy.10.count_ref, bf16[512,768]{1,0:T(8,128)(2,1)} %bitcast.9, bf16[512,768]{1,0:T(8,128)(2,1)} %bitcast.11, bf16[768,1152]{1,0:T(8,128)(2,1)} %qkv_hbm.3, ...), custom_call_target="tpu_custom_call" | custom-call | flops 4831838208 | bytes 30000000 | tf_op jit(solution)/shard_map/pallas_call | solution.py:325
  23.2 0.0 all-to-all-done
  23.2 0.1 reduce_sum.21
  23.3 26.5 %all_to_all.10 = bf16[48,3,128]{2,1,0:T(4,128)(2,1)S(1)} all-to-all(bf16[48,3,128]{2,1,0:T(4,128)(2,1)S(1)} %reshape.25), channel_id=1, replica_groups={{633,635,637,639,625,627,629,631,761,763,765,767,753,755,757,759,121,12..., dimensions={0} | all-to-all | bytes 73728 | tf_op jit(solution)/shard_map/all_to_all | solution.py:370
  49.8 0.6 %convert_reduce_fusion = f32[3,128]{1,0:T(4,128)} fusion(bf16[48,3,128]{2,1,0:T(4,128)(2,1)S(1)} %all_to_all.10), kind=kLoop, calls=%fused_computation | loop fusion | flops 36480 | bytes 38400 | tf_op jit(solution)/shard_map/reduce_sum | solution.py:371
  (1 shorter events, 0.0 us)
Async XLA Ops:
  6.7 16.5 %all-to-all-start = ((bf16[16,144,128]{2,1,0:T(8,128)(2,1)}), bf16[16,144,128]{2,1,0:T(8,128)(2,1)S(1)}, u32[]{:S(2)}, u32[]{:S(2)}) async-start(bf16[16,144,128]{2,1,0:T(8,128)(2,1)} %shard_map.94), calls=%async_computation | async-start | bytes 1179648 | tf_op jit(solution)/shard_map/all_to_all | solution.py:366

commit v5 on v4

--- a/solution.py
+++ b/solution.py
@@ -42,6 +42,10 @@
 def turned_by(array, first, axis):
     before, after = jnp.split(array, [first], axis)
     return jnp.concatenate([after, before], axis)
+
+
+def downward(count):
+    return [(FIRST_Z - i) % count for i in range(count)]
 
 
 def keep_live(ref, count_ref, cells):
@@ -158,7 +162,7 @@
         for k in range(pairs):
             part = total_ref[k, pl.ds(core, width // 2, stride=2), :].reshape(zs * 4, ys, PAIR)
             part = turned_by(part, FIRST_Y, 1).reshape(zs // 2, 8, ys, PAIR)
-            part = turned_by(part, FIRST_Z, 0)
+            part = jnp.concatenate([part[z : z + 1] for z in downward(zs // 2)], 0)
             for column in range(8):
                 odd, xlo, xhi = column // 4, column // 2 % 2, column % 2
                 first = COLUMNS.index((xlo, xhi, core, odd)) * lines + k
@@ -358,7 +362,7 @@
         return ((((2 * half_z + odd) * 2 + xlo) * 2 + xhi) * ys + y) * 2 + core
 
     half = zs // 2
-    places = [((FIRST_Z + i) % half, (FIRST_Y + j) % ys) for i in range(half) for j in range(ys)]
+    places = [(z, (FIRST_Y + j) % ys) for z in downward(half) for j in range(ys)]
     near = [[device(*place, column) for column in COLUMNS] for place in places]
     far = [[device(*place, column) for place in places] for column in COLUMNS]
     share = share_call(x, g, wet, count, qkv_weight, score_bias, zs, ys)

time: 50.7 us -> 50.6 us (level)
  no operation moved by 1% of the time
where the time goes in v5:
time: 50.6 us; the launch traced here: 50.3 us
  blocking collectives  26.4 us (52%)
  Pallas kernels  14.4 us (28%)
  starting transfers between devices  7.48 us (15%)
  between operations  1.31 us (3%)
  other arithmetic  0.72 us (1%)
    all_to_all x1, blocking collectives, shards(): got = lax.all_to_all(part, both, 0, 0, tiled=True, axis_index_groups=far)  26.4 us
    pallas_call x1, Pallas kernels, grads_call(): pl.pallas_call(functools.partial(grads_kernel, sizes=sizes), out_shape=(f...  8.98 us
    all_to_all x1, starting transfers between devices, shards(): got = lax.all_to_all(share, both, 0, 0, tiled=True, axis_index_groups=near)  7.48 us
    pallas_call x1, Pallas kernels, share_call(): pl.pallas_call(functools.partial(share_kernel, sizes=sizes, zs=zs, ys=ys)...  5.41 us
  transfers between devices with their start and end apart: 1, of which 0 were waited for; matrix products, arithmetic and copies ran while one was open for 0% of the time, Pallas kernels for 18%

profile of v5, /device:TPU:8, one launch (start us, length us, event | category | flops | bytes accessed | tf_op | source)
XLA Modules:
  0.0 50.3 jit_solution(11967846342039789646)
XLA Ops:
  1.3 5.4 %shard_map.94 = bf16[16,144,128]{2,1,0:T(8,128)(2,1)} custom-call(s32[8,64]{1,0:T(8,128)} %bitcast.14, f32[384,64]{1,0:T(8,128)} %bitcast.12, s32[1,1]{1,0:T(1,128)S(6)} %copy.10.count_ref, bf16[512,768]{1,0:T(8,128)(2,1)} %bitcast.8, bf16[512,768]{1,0:T(8,128)(2,1)} %bitcast.10, bf16[768,1152]{1,0:T(8,128)(2,1)} %qkv_hbm.3), custom_call_target="tpu_custom_call" | custom-call | flops 1207959552 | bytes 4000000 | tf_op jit(solution)/shard_map/pallas_call | solution.py:302
  6.7 7.5 %all-to-all-start = ((bf16[16,144,128]{2,1,0:T(8,128)(2,1)}), bf16[16,144,128]{2,1,0:T(8,128)(2,1)S(1)}, u32[]{:S(2)}, u32[]{:S(2)}) async-start(bf16[16,144,128]{2,1,0:T(8,128)(2,1)} %shard_map.94), calls=%async_computation | async-start | bytes 1179648 | tf_op jit(solution)/shard_map/all_to_all | solution.py:370
  14.2 9.0 %shard_map.95 = (bf16[512,768]{1,0:T(8,128)(2,1)}, bf16[512,768]{1,0:T(8,128)(2,1)}) custom-call(s32[8,64]{1,0:T(8,128)} %bitcast.15, f32[384,64]{1,0:T(8,128)} %bitcast.13, s32[1,1]{1,0:T(1,128)S(6)} %copy.10.count_ref, bf16[512,768]{1,0:T(8,128)(2,1)} %bitcast.9, bf16[512,768]{1,0:T(8,128)(2,1)} %bitcast.11, bf16[768,1152]{1,0:T(8,128)(2,1)} %qkv_hbm.3, ...), custom_call_target="tpu_custom_call" | custom-call | flops 4831838208 | bytes 30000000 | tf_op jit(solution)/shard_map/pallas_call | solution.py:329
  23.2 0.0 all-to-all-done
  23.2 0.1 reduce_sum.21
  23.3 26.4 %all_to_all.10 = bf16[48,3,128]{2,1,0:T(4,128)(2,1)S(1)} all-to-all(bf16[48,3,128]{2,1,0:T(4,128)(2,1)S(1)} %reshape.25), channel_id=1, replica_groups={{633,635,637,639,625,627,629,631,505,507,509,511,497,499,501,503,377,37..., dimensions={0} | all-to-all | bytes 73728 | tf_op jit(solution)/shard_map/all_to_all | solution.py:374
  49.7 0.6 %convert_reduce_fusion = f32[3,128]{1,0:T(4,128)} fusion(bf16[48,3,128]{2,1,0:T(4,128)(2,1)S(1)} %all_to_all.10), kind=kLoop, calls=%fused_computation | loop fusion | flops 36480 | bytes 38400 | tf_op jit(solution)/shard_map/reduce_sum | solution.py:375
  (1 shorter events, 0.0 us)
Async XLA Ops:
  6.7 16.5 %all-to-all-start = ((bf16[16,144,128]{2,1,0:T(8,128)(2,1)}), bf16[16,144,128]{2,1,0:T(8,128)(2,1)S(1)}, u32[]{:S(2)}, u32[]{:S(2)}) async-start(bf16[16,144,128]{2,1,0:T(8,128)(2,1)} %shard_map.94), calls=%async_computation | async-start | bytes 1179648 | tf_op jit(solution)/shard_map/all_to_all | solution.py:370
